TPU v7x, 512 devices: a whole 4x8x8 slice. The times are simulated.
512 devices in a mesh: loop: 32 (over y_hi, x, core), grp: 16 (over y_lo, z).
Axes of the slice: x: 4, y: 8 (y_hi: 4, y_lo: 2; y = y_hi * 2 + y_lo), z: 8, core: 2. Of those that a mesh axis runs over, the one named last changes fastest.
Arguments:
- image_emb: bfloat16 [8192, 1152], P(('loop', 'grp')), may hold values from -6 to 6
- text_emb: bfloat16 [8192, 1152], P(('loop', 'grp')), may hold values from -6 to 6
- log_scale: float32 [1], replicated, may hold values from 4.2 to 4.8
- bias: float32 [1], replicated, may hold values from -4 to -2
Outputs:
- image_grad: float32 [8192, 1152], P(('loop', 'grp'))
- text_grad: float32 [8192, 1152], P(('loop', 'grp'))
All inputs are finite; a program needn't handle non-finite values.
Results may differ from a plain program's by a relative error of at most 0.008.
Values may be sent and summed in bfloat16 or wider, within the bound.
A program may use at most 64 MiB of HBM per device.

v0:
```python
import jax
import jax.numpy as jnp
from jax import lax
from jax.sharding import PartitionSpec as P

EPS = 1e-06


def from_behind(value, axis, steps):
    count = lax.axis_size(axis)
    pairs = [(source, (source + steps) % count) for source in range(count)]
    return lax.ppermute(value, axis, pairs)


def normalize(values):
    wide = values.astype(jnp.float32)
    length = jnp.sqrt(jnp.sum(wide * wide, axis=-1, keepdims=True) + EPS)
    return (wide / length, length)


def norm_back(unit_rows, length, upstream):
    along = jnp.sum(unit_rows * upstream, axis=-1, keepdims=True)
    return (upstream - unit_rows * along) / length


def move_text(text_rows):
    return from_behind(text_rows, "loop", 1)


def move_grads(text_grad):
    return from_behind(text_grad, "loop", 1)


def per_device(image_emb, text_emb, log_scale, bias):
    row_count, feat_width = image_emb.shape
    loop_count = lax.axis_size("loop")
    groups = lax.axis_size("grp")
    loop_at = lax.axis_index("loop")
    group_at = lax.axis_index("grp")
    logit_scale = jnp.exp(log_scale[0])
    offset = bias[0]
    img_unit, img_length = normalize(image_emb)
    txt_unit, txt_length = normalize(text_emb)
    image_block = lax.all_gather(img_unit.astype(jnp.bfloat16), "grp", axis=0, tiled=True)
    block_rows = groups * row_count
    image_ids = loop_at * block_rows + jnp.arange(block_rows, dtype=jnp.int32)
    text_rows = txt_unit.astype(jnp.bfloat16)

    def text_ids(turn_index):
        source = (loop_at - turn_index) % loop_count
        return (source * groups + group_at) * row_count + jnp.arange(row_count, dtype=jnp.int32)

    def station(turn_index, moving, summed, grads_seen, texts_seen):
        logits = (
            logit_scale
            * jnp.einsum("id,kd->ik", image_block, moving, preferred_element_type=jnp.float32)
            + offset
        )
        labels = (image_ids[:, None] == text_ids(turn_index)[None, :]).astype(jnp.float32)
        grad_low = (logit_scale * (jax.nn.sigmoid(logits) - labels)).astype(jnp.bfloat16)
        summed = summed + jnp.einsum(
            "ik,id->kd", grad_low, image_block, preferred_element_type=jnp.float32
        )
        grads_seen = lax.dynamic_update_slice(grads_seen, grad_low, (0, turn_index * row_count))
        texts_seen = lax.dynamic_update_slice(texts_seen, moving, (turn_index * row_count, 0))
        return (summed, grads_seen, texts_seen)

    text_grad = jnp.zeros((row_count, feat_width), jnp.float32)
    grad_table = jnp.zeros((block_rows, loop_count * row_count), jnp.bfloat16)
    text_table = jnp.zeros((loop_count * row_count, feat_width), jnp.bfloat16)
    text_grad, grad_table, text_table = station(
        jnp.int32(0), text_rows, text_grad, grad_table, text_table
    )

    def turn(turn_index, loop_state):
        moving, summed, grads_seen, texts_seen = loop_state
        moving = move_text(moving)
        summed = move_grads(summed)
        summed, grads_seen, texts_seen = station(turn_index, moving, summed, grads_seen, texts_seen)
        return (moving, summed, grads_seen, texts_seen)

    text_rows, text_grad, grad_table, text_table = lax.fori_loop(
        1, loop_count, turn, (text_rows, text_grad, grad_table, text_table)
    )
    text_grad = move_grads(text_grad)
    image_terms = jnp.dot(grad_table, text_table, preferred_element_type=jnp.float32)
    image_sum = lax.psum_scatter(image_terms, "grp", scatter_dimension=0, tiled=True)
    return (norm_back(img_unit, img_length, image_sum), norm_back(txt_unit, txt_length, text_grad))


def solution(mesh):
    return jax.shard_map(
        per_device,
        mesh=mesh,
        in_specs=(P(("loop", "grp"), None), P(("loop", "grp"), None), P(), P()),
        out_specs=(P(("loop", "grp"), None), P(("loop", "grp"), None)),
        check_vma=False,
    )
```

profile of v0, /device:TPU:4, one launch (start us, length us, event | category | flops | bytes accessed | tf_op | source)
XLA Modules:
  0.0 511.3 jit_solution(7196596203872255199)
XLA Ops:
  12.1 42.7 %all_gather.3 = bf16[256,1152]{1,0:T(8,128)(2,1)S(1)} all-gather(bf16[16,1152]{1,0:T(8,128)(2,1)S(1)} %fusion.21), channel_id=1, replica_groups=mesh['loop'=32,'grp'=16] {'grp'}, dimensions={0}, use_global_device_ids=true | all-gather | bytes 626688 | tf_op jit(solution)/shard_map/all_gather | solution.py:44
  55.4 350.3 %while.22 = (s32[]{:T(128)}, bf16[16,1152]{1,0:T(8,128)(2,1)S(1)}, f32[16,1152]{1,0:T(8,128)S(1)}, bf16[256,512]{0,1:T(8,128)(2,1)S(1)}, bf16[512,1152]{1,0:T(8,...) while((s32[]{:T(128)}, bf16[16,1152]{1,0:T(8,128)(2,1)S(1)}, ...), condition=%wide.region_3.4_spmd.clone, body=%wide.region_2.3_spmd.clone.sunk | while | flops 18934052 | bytes 1981456 | solution.py:82
  73.0 6.9 %collective-permute-start.1 = (f32[16,1152]{1,0:T(8,128)S(1)}, f32[16,1152]{1,0:T(8,128)S(1)}, u32[]{:S(2)}, u32[]{:S(2)}) collective-permute-start(f32[16,1152]{1,0:T(8,128)S(1)} %get-tuple-element.411), channel_id=1, source_target_pairs={{0,16},{16,32},{32,48},{48,64},{64,80},{80,96},{96,112},{112,128},... | collective-permute-start | bytes 221192 | tf_op jit(solution)/shard_map/while/body/eval_jaxpr/ppermute | solution.py:12
  83.7 7.8 %collective-permute-start.1 = (f32[16,1152]{1,0:T(8,128)S(1)}, f32[16,1152]{1,0:T(8,128)S(1)}, u32[]{:S(2)}, u32[]{:S(2)}) collective-permute-start(f32[16,1152]{1,0:T(8,128)S(1)} %get-tuple-element.411), channel_id=1, source_target_pairs={{0,16},{16,32},{32,48},{48,64},{64,80},{80,96},{96,112},{112,128},... | collective-permute-start | bytes 221192 | tf_op jit(solution)/shard_map/while/body/eval_jaxpr/ppermute | solution.py:12
  95.3 7.0 %collective-permute-start.1 = (f32[16,1152]{1,0:T(8,128)S(1)}, f32[16,1152]{1,0:T(8,128)S(1)}, u32[]{:S(2)}, u32[]{:S(2)}) collective-permute-start(f32[16,1152]{1,0:T(8,128)S(1)} %get-tuple-element.411), channel_id=1, source_target_pairs={{0,16},{16,32},{32,48},{48,64},{64,80},{80,96},{96,112},{112,128},... | collective-permute-start | bytes 221192 | tf_op jit(solution)/shard_map/while/body/eval_jaxpr/ppermute | solution.py:12
  106.4 7.1 %collective-permute-start.1 = (f32[16,1152]{1,0:T(8,128)S(1)}, f32[16,1152]{1,0:T(8,128)S(1)}, u32[]{:S(2)}, u32[]{:S(2)}) collective-permute-start(f32[16,1152]{1,0:T(8,128)S(1)} %get-tuple-element.411), channel_id=1, source_target_pairs={{0,16},{16,32},{32,48},{48,64},{64,80},{80,96},{96,112},{112,128},... | collective-permute-start | bytes 221192 | tf_op jit(solution)/shard_map/while/body/eval_jaxpr/ppermute | solution.py:12
  117.4 7.0 %collective-permute-start.1 = (f32[16,1152]{1,0:T(8,128)S(1)}, f32[16,1152]{1,0:T(8,128)S(1)}, u32[]{:S(2)}, u32[]{:S(2)}) collective-permute-start(f32[16,1152]{1,0:T(8,128)S(1)} %get-tuple-element.411), channel_id=1, source_target_pairs={{0,16},{16,32},{32,48},{48,64},{64,80},{80,96},{96,112},{112,128},... | collective-permute-start | bytes 221192 | tf_op jit(solution)/shard_map/while/body/eval_jaxpr/ppermute | solution.py:12
  128.2 7.0 %collective-permute-start.1 = (f32[16,1152]{1,0:T(8,128)S(1)}, f32[16,1152]{1,0:T(8,128)S(1)}, u32[]{:S(2)}, u32[]{:S(2)}) collective-permute-start(f32[16,1152]{1,0:T(8,128)S(1)} %get-tuple-element.411), channel_id=1, source_target_pairs={{0,16},{16,32},{32,48},{48,64},{64,80},{80,96},{96,112},{112,128},... | collective-permute-start | bytes 221192 | tf_op jit(solution)/shard_map/while/body/eval_jaxpr/ppermute | solution.py:12
  139.0 7.0 %collective-permute-start.1 = (f32[16,1152]{1,0:T(8,128)S(1)}, f32[16,1152]{1,0:T(8,128)S(1)}, u32[]{:S(2)}, u32[]{:S(2)}) collective-permute-start(f32[16,1152]{1,0:T(8,128)S(1)} %get-tuple-element.411), channel_id=1, source_target_pairs={{0,16},{16,32},{32,48},{48,64},{64,80},{80,96},{96,112},{112,128},... | collective-permute-start | bytes 221192 | tf_op jit(solution)/shard_map/while/body/eval_jaxpr/ppermute | solution.py:12
  149.8 7.0 %collective-permute-start.1 = (f32[16,1152]{1,0:T(8,128)S(1)}, f32[16,1152]{1,0:T(8,128)S(1)}, u32[]{:S(2)}, u32[]{:S(2)}) collective-permute-start(f32[16,1152]{1,0:T(8,128)S(1)} %get-tuple-element.411), channel_id=1, source_target_pairs={{0,16},{16,32},{32,48},{48,64},{64,80},{80,96},{96,112},{112,128},... | collective-permute-start | bytes 221192 | tf_op jit(solution)/shard_map/while/body/eval_jaxpr/ppermute | solution.py:12
  160.6 7.0 %collective-permute-start.1 = (f32[16,1152]{1,0:T(8,128)S(1)}, f32[16,1152]{1,0:T(8,128)S(1)}, u32[]{:S(2)}, u32[]{:S(2)}) collective-permute-start(f32[16,1152]{1,0:T(8,128)S(1)} %get-tuple-element.411), channel_id=1, source_target_pairs={{0,16},{16,32},{32,48},{48,64},{64,80},{80,96},{96,112},{112,128},... | collective-permute-start | bytes 221192 | tf_op jit(solution)/shard_map/while/body/eval_jaxpr/ppermute | solution.py:12
  171.5 7.0 %collective-permute-start.1 = (f32[16,1152]{1,0:T(8,128)S(1)}, f32[16,1152]{1,0:T(8,128)S(1)}, u32[]{:S(2)}, u32[]{:S(2)}) collective-permute-start(f32[16,1152]{1,0:T(8,128)S(1)} %get-tuple-element.411), channel_id=1, source_target_pairs={{0,16},{16,32},{32,48},{48,64},{64,80},{80,96},{96,112},{112,128},... | collective-permute-start | bytes 221192 | tf_op jit(solution)/shard_map/while/body/eval_jaxpr/ppermute | solution.py:12
  182.3 7.0 %collective-permute-start.1 = (f32[16,1152]{1,0:T(8,128)S(1)}, f32[16,1152]{1,0:T(8,128)S(1)}, u32[]{:S(2)}, u32[]{:S(2)}) collective-permute-start(f32[16,1152]{1,0:T(8,128)S(1)} %get-tuple-element.411), channel_id=1, source_target_pairs={{0,16},{16,32},{32,48},{48,64},{64,80},{80,96},{96,112},{112,128},... | collective-permute-start | bytes 221192 | tf_op jit(solution)/shard_map/while/body/eval_jaxpr/ppermute | solution.py:12
  193.7 7.1 %collective-permute-start.1 = (f32[16,1152]{1,0:T(8,128)S(1)}, f32[16,1152]{1,0:T(8,128)S(1)}, u32[]{:S(2)}, u32[]{:S(2)}) collective-permute-start(f32[16,1152]{1,0:T(8,128)S(1)} %get-tuple-element.411), channel_id=1, source_target_pairs={{0,16},{16,32},{32,48},{48,64},{64,80},{80,96},{96,112},{112,128},... | collective-permute-start | bytes 221192 | tf_op jit(solution)/shard_map/while/body/eval_jaxpr/ppermute | solution.py:12
  204.6 7.8 %collective-permute-start.1 = (f32[16,1152]{1,0:T(8,128)S(1)}, f32[16,1152]{1,0:T(8,128)S(1)}, u32[]{:S(2)}, u32[]{:S(2)}) collective-permute-start(f32[16,1152]{1,0:T(8,128)S(1)} %get-tuple-element.411), channel_id=1, source_target_pairs={{0,16},{16,32},{32,48},{48,64},{64,80},{80,96},{96,112},{112,128},... | collective-permute-start | bytes 221192 | tf_op jit(solution)/shard_map/while/body/eval_jaxpr/ppermute | solution.py:12
  216.2 7.0 %collective-permute-start.1 = (f32[16,1152]{1,0:T(8,128)S(1)}, f32[16,1152]{1,0:T(8,128)S(1)}, u32[]{:S(2)}, u32[]{:S(2)}) collective-permute-start(f32[16,1152]{1,0:T(8,128)S(1)} %get-tuple-element.411), channel_id=1, source_target_pairs={{0,16},{16,32},{32,48},{48,64},{64,80},{80,96},{96,112},{112,128},... | collective-permute-start | bytes 221192 | tf_op jit(solution)/shard_map/while/body/eval_jaxpr/ppermute | solution.py:12
  227.0 7.0 %collective-permute-start.1 = (f32[16,1152]{1,0:T(8,128)S(1)}, f32[16,1152]{1,0:T(8,128)S(1)}, u32[]{:S(2)}, u32[]{:S(2)}) collective-permute-start(f32[16,1152]{1,0:T(8,128)S(1)} %get-tuple-element.411), channel_id=1, source_target_pairs={{0,16},{16,32},{32,48},{48,64},{64,80},{80,96},{96,112},{112,128},... | collective-permute-start | bytes 221192 | tf_op jit(solution)/shard_map/while/body/eval_jaxpr/ppermute | solution.py:12
  238.6 6.2 %collective-permute-start.1 = (f32[16,1152]{1,0:T(8,128)S(1)}, f32[16,1152]{1,0:T(8,128)S(1)}, u32[]{:S(2)}, u32[]{:S(2)}) collective-permute-start(f32[16,1152]{1,0:T(8,128)S(1)} %get-tuple-element.411), channel_id=1, source_target_pairs={{0,16},{16,32},{32,48},{48,64},{64,80},{80,96},{96,112},{112,128},... | collective-permute-start | bytes 221192 | tf_op jit(solution)/shard_map/while/body/eval_jaxpr/ppermute | solution.py:12
  250.7 5.1 collective-permute-start.1
  374.5 4.6 collective-permute-done
  386.6 4.6 collective-permute-done
  398.6 4.6 collective-permute-done
  409.2 8.1 %collective-permute-done.2 = f32[16,1152]{1,0:T(8,128)S(1)} collective-permute-done((f32[16,1152]{1,0:T(8,128)S(1)}, f32[16,1152]{1,0:T(8,128)S(1)}, u32[]{:S(2)}, u32[]{:S(2)}) %collective-permute-start.2) | collective-permute-done | bytes 73760 | tf_op jit(solution)/shard_map/ppermute | solution.py:12
  418.3 83.5 %reduce-scatter.2.cloned.1.call-done = f32[16,1152]{1,0:T(8,128)} async-done(((f32[256,1152]{1,0:T(8,128)}), f32[16,1152]{1,0:T(8,128)}) %reduce-scatter.2.cloned.1.call-update) | async-done | bytes 73744 | tf_op jit(solution)/shard_map/reduce_scatter | solution.py:87
  (314 shorter events, 226.8 us)
Async XLA Ops:
  7.2 494.6 %reduce-scatter.2.cloned.1.call-start = ((), (), s32[]{:S(2)}) async-start(), calls=%async_computation.1 | async-start | bytes 1253376 | tf_op jit(solution)/shard_map/reduce_scatter | solution.py:87
  81.2 10.4 %collective-permute-start = (bf16[16,1152]{1,0:T(8,128)(2,1)S(1)}, bf16[16,1152]{1,0:T(8,128)(2,1)S(1)}, u32[]{:S(2)}, u32[]{:S(2)}) collective-permute-start(bf16[16,1152]{1,0:T(8,128)(2,1)S(1)} %get-tuple-element.410), channel_id=1, source_target_pairs={{0,16},{16,32},{32,48},{48,64},{64,80},{80,96},{96,112},{112,128},... | collective-permute-start | bytes 110600 | tf_op jit(solution)/shard_map/while/body/eval_jaxpr/ppermute | solution.py:12
  92.8 9.6 %collective-permute-start = (bf16[16,1152]{1,0:T(8,128)(2,1)S(1)}, bf16[16,1152]{1,0:T(8,128)(2,1)S(1)}, u32[]{:S(2)}, u32[]{:S(2)}) collective-permute-start(bf16[16,1152]{1,0:T(8,128)(2,1)S(1)} %get-tuple-element.410), channel_id=1, source_target_pairs={{0,16},{16,32},{32,48},{48,64},{64,80},{80,96},{96,112},{112,128},... | collective-permute-start | bytes 110600 | tf_op jit(solution)/shard_map/while/body/eval_jaxpr/ppermute | solution.py:12
  103.6 10.0 %collective-permute-start = (bf16[16,1152]{1,0:T(8,128)(2,1)S(1)}, bf16[16,1152]{1,0:T(8,128)(2,1)S(1)}, u32[]{:S(2)}, u32[]{:S(2)}) collective-permute-start(bf16[16,1152]{1,0:T(8,128)(2,1)S(1)} %get-tuple-element.410), channel_id=1, source_target_pairs={{0,16},{16,32},{32,48},{48,64},{64,80},{80,96},{96,112},{112,128},... | collective-permute-start | bytes 110600 | tf_op jit(solution)/shard_map/while/body/eval_jaxpr/ppermute | solution.py:12
  114.8 9.6 %collective-permute-start = (bf16[16,1152]{1,0:T(8,128)(2,1)S(1)}, bf16[16,1152]{1,0:T(8,128)(2,1)S(1)}, u32[]{:S(2)}, u32[]{:S(2)}) collective-permute-start(bf16[16,1152]{1,0:T(8,128)(2,1)S(1)} %get-tuple-element.410), channel_id=1, source_target_pairs={{0,16},{16,32},{32,48},{48,64},{64,80},{80,96},{96,112},{112,128},... | collective-permute-start | bytes 110600 | tf_op jit(solution)/shard_map/while/body/eval_jaxpr/ppermute | solution.py:12
  190.5 10.3 %collective-permute-start = (bf16[16,1152]{1,0:T(8,128)(2,1)S(1)}, bf16[16,1152]{1,0:T(8,128)(2,1)S(1)}, u32[]{:S(2)}, u32[]{:S(2)}) collective-permute-start(bf16[16,1152]{1,0:T(8,128)(2,1)S(1)} %get-tuple-element.410), channel_id=1, source_target_pairs={{0,16},{16,32},{32,48},{48,64},{64,80},{80,96},{96,112},{112,128},... | collective-permute-start | bytes 110600 | tf_op jit(solution)/shard_map/while/body/eval_jaxpr/ppermute | solution.py:12
  202.0 10.4 %collective-permute-start = (bf16[16,1152]{1,0:T(8,128)(2,1)S(1)}, bf16[16,1152]{1,0:T(8,128)(2,1)S(1)}, u32[]{:S(2)}, u32[]{:S(2)}) collective-permute-start(bf16[16,1152]{1,0:T(8,128)(2,1)S(1)} %get-tuple-element.410), channel_id=1, source_target_pairs={{0,16},{16,32},{32,48},{48,64},{64,80},{80,96},{96,112},{112,128},... | collective-permute-start | bytes 110600 | tf_op jit(solution)/shard_map/while/body/eval_jaxpr/ppermute | solution.py:12
  238.6 9.9 %collective-permute-start.1 = (f32[16,1152]{1,0:T(8,128)S(1)}, f32[16,1152]{1,0:T(8,128)S(1)}, u32[]{:S(2)}, u32[]{:S(2)}) collective-permute-start(f32[16,1152]{1,0:T(8,128)S(1)} %get-tuple-element.411), channel_id=1, source_target_pairs={{0,16},{16,32},{32,48},{48,64},{64,80},{80,96},{96,112},{112,128},... | collective-permute-start | bytes 221192 | tf_op jit(solution)/shard_map/while/body/eval_jaxpr/ppermute | solution.py:12
  250.7 9.9 %collective-permute-start.1 = (f32[16,1152]{1,0:T(8,128)S(1)}, f32[16,1152]{1,0:T(8,128)S(1)}, u32[]{:S(2)}, u32[]{:S(2)}) collective-permute-start(f32[16,1152]{1,0:T(8,128)S(1)} %get-tuple-element.411), channel_id=1, source_target_pairs={{0,16},{16,32},{32,48},{48,64},{64,80},{80,96},{96,112},{112,128},... | collective-permute-start | bytes 221192 | tf_op jit(solution)/shard_map/while/body/eval_jaxpr/ppermute | solution.py:12
  262.7 9.9 %collective-permute-start.1 = (f32[16,1152]{1,0:T(8,128)S(1)}, f32[16,1152]{1,0:T(8,128)S(1)}, u32[]{:S(2)}, u32[]{:S(2)}) collective-permute-start(f32[16,1152]{1,0:T(8,128)S(1)} %get-tuple-element.411), channel_id=1, source_target_pairs={{0,16},{16,32},{32,48},{48,64},{64,80},{80,96},{96,112},{112,128},... | collective-permute-start | bytes 221192 | tf_op jit(solution)/shard_map/while/body/eval_jaxpr/ppermute | solution.py:12
  274.7 9.9 %collective-permute-start.1 = (f32[16,1152]{1,0:T(8,128)S(1)}, f32[16,1152]{1,0:T(8,128)S(1)}, u32[]{:S(2)}, u32[]{:S(2)}) collective-permute-start(f32[16,1152]{1,0:T(8,128)S(1)} %get-tuple-element.411), channel_id=1, source_target_pairs={{0,16},{16,32},{32,48},{48,64},{64,80},{80,96},{96,112},{112,128},... | collective-permute-start | bytes 221192 | tf_op jit(solution)/shard_map/while/body/eval_jaxpr/ppermute | solution.py:12
  286.8 9.9 %collective-permute-start.1 = (f32[16,1152]{1,0:T(8,128)S(1)}, f32[16,1152]{1,0:T(8,128)S(1)}, u32[]{:S(2)}, u32[]{:S(2)}) collective-permute-start(f32[16,1152]{1,0:T(8,128)S(1)} %get-tuple-element.411), channel_id=1, source_target_pairs={{0,16},{16,32},{32,48},{48,64},{64,80},{80,96},{96,112},{112,128},... | collective-permute-start | bytes 221192 | tf_op jit(solution)/shard_map/while/body/eval_jaxpr/ppermute | solution.py:12
  298.8 9.9 %collective-permute-start.1 = (f32[16,1152]{1,0:T(8,128)S(1)}, f32[16,1152]{1,0:T(8,128)S(1)}, u32[]{:S(2)}, u32[]{:S(2)}) collective-permute-start(f32[16,1152]{1,0:T(8,128)S(1)} %get-tuple-element.411), channel_id=1, source_target_pairs={{0,16},{16,32},{32,48},{48,64},{64,80},{80,96},{96,112},{112,128},... | collective-permute-start | bytes 221192 | tf_op jit(solution)/shard_map/while/body/eval_jaxpr/ppermute | solution.py:12
  308.9 9.8 %collective-permute-start = (bf16[16,1152]{1,0:T(8,128)(2,1)S(1)}, bf16[16,1152]{1,0:T(8,128)(2,1)S(1)}, u32[]{:S(2)}, u32[]{:S(2)}) collective-permute-start(bf16[16,1152]{1,0:T(8,128)(2,1)S(1)} %get-tuple-element.410), channel_id=1, source_target_pairs={{0,16},{16,32},{32,48},{48,64},{64,80},{80,96},{96,112},{112,128},... | collective-permute-start | bytes 110600 | tf_op jit(solution)/shard_map/while/body/eval_jaxpr/ppermute | solution.py:12
  310.8 10.2 %collective-permute-start.1 = (f32[16,1152]{1,0:T(8,128)S(1)}, f32[16,1152]{1,0:T(8,128)S(1)}, u32[]{:S(2)}, u32[]{:S(2)}) collective-permute-start(f32[16,1152]{1,0:T(8,128)S(1)} %get-tuple-element.411), channel_id=1, source_target_pairs={{0,16},{16,32},{32,48},{48,64},{64,80},{80,96},{96,112},{112,128},... | collective-permute-start | bytes 221192 | tf_op jit(solution)/shard_map/while/body/eval_jaxpr/ppermute | solution.py:12
  323.1 9.9 %collective-permute-start.1 = (f32[16,1152]{1,0:T(8,128)S(1)}, f32[16,1152]{1,0:T(8,128)S(1)}, u32[]{:S(2)}, u32[]{:S(2)}) collective-permute-start(f32[16,1152]{1,0:T(8,128)S(1)} %get-tuple-element.411), channel_id=1, source_target_pairs={{0,16},{16,32},{32,48},{48,64},{64,80},{80,96},{96,112},{112,128},... | collective-permute-start | bytes 221192 | tf_op jit(solution)/shard_map/while/body/eval_jaxpr/ppermute | solution.py:12
  335.2 9.9 %collective-permute-start.1 = (f32[16,1152]{1,0:T(8,128)S(1)}, f32[16,1152]{1,0:T(8,128)S(1)}, u32[]{:S(2)}, u32[]{:S(2)}) collective-permute-start(f32[16,1152]{1,0:T(8,128)S(1)} %get-tuple-element.411), channel_id=1, source_target_pairs={{0,16},{16,32},{32,48},{48,64},{64,80},{80,96},{96,112},{112,128},... | collective-permute-start | bytes 221192 | tf_op jit(solution)/shard_map/while/body/eval_jaxpr/ppermute | solution.py:12
  347.2 9.9 %collective-permute-start.1 = (f32[16,1152]{1,0:T(8,128)S(1)}, f32[16,1152]{1,0:T(8,128)S(1)}, u32[]{:S(2)}, u32[]{:S(2)}) collective-permute-start(f32[16,1152]{1,0:T(8,128)S(1)} %get-tuple-element.411), channel_id=1, source_target_pairs={{0,16},{16,32},{32,48},{48,64},{64,80},{80,96},{96,112},{112,128},... | collective-permute-start | bytes 221192 | tf_op jit(solution)/shard_map/while/body/eval_jaxpr/ppermute | solution.py:12
  357.3 9.7 %collective-permute-start = (bf16[16,1152]{1,0:T(8,128)(2,1)S(1)}, bf16[16,1152]{1,0:T(8,128)(2,1)S(1)}, u32[]{:S(2)}, u32[]{:S(2)}) collective-permute-start(bf16[16,1152]{1,0:T(8,128)(2,1)S(1)} %get-tuple-element.410), channel_id=1, source_target_pairs={{0,16},{16,32},{32,48},{48,64},{64,80},{80,96},{96,112},{112,128},... | collective-permute-start | bytes 110600 | tf_op jit(solution)/shard_map/while/body/eval_jaxpr/ppermute | solution.py:12
  359.2 10.1 %collective-permute-start.1 = (f32[16,1152]{1,0:T(8,128)S(1)}, f32[16,1152]{1,0:T(8,128)S(1)}, u32[]{:S(2)}, u32[]{:S(2)}) collective-permute-start(f32[16,1152]{1,0:T(8,128)S(1)} %get-tuple-element.411), channel_id=1, source_target_pairs={{0,16},{16,32},{32,48},{48,64},{64,80},{80,96},{96,112},{112,128},... | collective-permute-start | bytes 221192 | tf_op jit(solution)/shard_map/while/body/eval_jaxpr/ppermute | solution.py:12
  371.5 10.0 %collective-permute-start.1 = (f32[16,1152]{1,0:T(8,128)S(1)}, f32[16,1152]{1,0:T(8,128)S(1)}, u32[]{:S(2)}, u32[]{:S(2)}) collective-permute-start(f32[16,1152]{1,0:T(8,128)S(1)} %get-tuple-element.411), channel_id=1, source_target_pairs={{0,16},{16,32},{32,48},{48,64},{64,80},{80,96},{96,112},{112,128},... | collective-permute-start | bytes 221192 | tf_op jit(solution)/shard_map/while/body/eval_jaxpr/ppermute | solution.py:12
  383.6 9.9 %collective-permute-start.1 = (f32[16,1152]{1,0:T(8,128)S(1)}, f32[16,1152]{1,0:T(8,128)S(1)}, u32[]{:S(2)}, u32[]{:S(2)}) collective-permute-start(f32[16,1152]{1,0:T(8,128)S(1)} %get-tuple-element.411), channel_id=1, source_target_pairs={{0,16},{16,32},{32,48},{48,64},{64,80},{80,96},{96,112},{112,128},... | collective-permute-start | bytes 221192 | tf_op jit(solution)/shard_map/while/body/eval_jaxpr/ppermute | solution.py:12
  395.6 9.9 %collective-permute-start.1 = (f32[16,1152]{1,0:T(8,128)S(1)}, f32[16,1152]{1,0:T(8,128)S(1)}, u32[]{:S(2)}, u32[]{:S(2)}) collective-permute-start(f32[16,1152]{1,0:T(8,128)S(1)} %get-tuple-element.411), channel_id=1, source_target_pairs={{0,16},{16,32},{32,48},{48,64},{64,80},{80,96},{96,112},{112,128},... | collective-permute-start | bytes 221192 | tf_op jit(solution)/shard_map/while/body/eval_jaxpr/ppermute | solution.py:12
  407.3 10.0 %collective-permute-start.2 = (f32[16,1152]{1,0:T(8,128)S(1)}, f32[16,1152]{1,0:T(8,128)S(1)}, u32[]{:S(2)}, u32[]{:S(2)}) collective-permute-start(f32[16,1152]{1,0:T(8,128)S(1)} %get-tuple-element.271), channel_id=1, source_target_pairs={{0,16},{16,32},{32,48},{48,64},{64,80},{80,96},{96,112},{112,128},... | collective-permute-start | bytes 221192 | tf_op jit(solution)/shard_map/ppermute | solution.py:12
  (42 other events, 450.0 us)
Sparse Core Ops, SparseCore 0:
  407.4 94.3 reduce-scatter.1
where the time goes:
time: 514 us; the launch traced here: 511 us
  starting transfers between devices  234 us (46%)
  waiting for transfers between devices  170 us (33%)
  blocking collectives  42.7 us (8%)
  matrix products  37.2 us (7%)
  between operations  15.4 us (3%)
  other arithmetic  7.44 us (1%)
    ppermute x63, starting transfers between devices, from_behind(): return lax.ppermute(value, axis, pairs)  234 us
    ppermute x63, waiting for transfers between devices, from_behind(): return lax.ppermute(value, axis, pairs)  86.4 us
    reduce_scatter x1, waiting for transfers between devices, per_device(): lax.psum_scatter(image_terms, 'grp', scatter_dimension=0, tiled=True)  83.5 us
    all_gather x1, blocking collectives, per_device(): lax.all_gather(img_unit.astype(jnp.bfloat16), 'grp', axis=0, tiled=True)  42.7 us
    dot_general x32, matrix products, station(): jnp.einsum('id,kd->ik', image_block, moving, preferred_element_type=jnp.f...  29.5 us
  transfers between devices with their start and end apart: 64, of which 37 were waited for; matrix products, arithmetic and copies ran while one was open for 6% of the time, Pallas kernels for 0%

commit v1 on v0

v1 whole, which is shorter than its diff:
```python
import jax
import jax.numpy as jnp
from jax import lax
from jax.experimental import pallas as pl
from jax.experimental.pallas import tpu as pltpu
from jax.sharding import PartitionSpec as P

EPS = 1e-06
ROWS = 16
RING = 8
OFFS = (4, 3, -3, 2, -2, 1, -1, 0)
OWN = 7
HALF = RING * ROWS
BF = jnp.bfloat16
F32 = jnp.float32


def slot_of(offset):
    return OFFS.index(4 if offset in (4, -4) else offset)


GZ, GY, GXI, GXT, GC = 0, 8, 16, 24, 32
RC, RXI, RXT, RZ, RY = 48, 52, 56, 60, 68
NSEM = 76
BATCH = 2
NBATCH = RING // BATCH


def kernel(
    img_hbm, txt_hbm, scale_ref, bias_ref, out_i, out_t,
    raw, unit, length, img, txt, grad, own_i, own_t,
    snd_c, snd_xi, snd_xt, snd_z, snd_y,
    rcv_c, rcv_xi, rcv_xt, rcv_z, rcv_y,
    in_sem, ssem, rsem,
):
    loop_at = lax.axis_index("loop")
    grp_at = lax.axis_index("grp")
    c = loop_at % 2
    x = (loop_at // 2) % 4
    y_hi = loop_at // 8
    y_lo = grp_at // 8
    z = grp_at % 8
    y = y_hi * 2 + y_lo

    def device(dx, dy, dz, dc):
        return {"loop": ((dy // 2) * 4 + dx) * 2 + dc, "grp": (dy % 2) * 8 + dz}

    z_peer = {o: device(x, y, (z + o + RING) % RING, c) for o in OFFS if o}
    y_peer = {o: device(x, (y + o + RING) % RING, z, c) for o in OFFS if o}
    xa_peer = device(x + 1 - 2 * (x % 2), y, z, c)
    xb_peer = device(3 - x, y, z, c)
    c_peer = device(x, y, z, 1 - c)

    barrier = pltpu.get_barrier_semaphore()
    peers = list(z_peer.values()) + list(y_peer.values()) + [xa_peer, xb_peer, c_peer]
    for peer in peers:
        pl.semaphore_signal(barrier, 1, device_id=peer, device_id_type=pl.DeviceIdType.MESH)

    loads = [
        pltpu.make_async_copy(img_hbm, raw.at[0], in_sem.at[0]),
        pltpu.make_async_copy(txt_hbm, raw.at[1], in_sem.at[1]),
    ]
    for load in loads:
        load.start()

    def rows(ref, quarter, slot, count=1):
        return ref.at[pl.ds(quarter * HALF + slot * ROWS, count * ROWS)]

    sent = []

    def send(src, dst, s_at, r_at, peer):
        copy = pltpu.make_async_remote_copy(
            src, dst, ssem.at[s_at], rsem.at[r_at],
            device_id=peer, device_id_type=pl.DeviceIdType.MESH,
        )
        copy.start()
        sent.append(copy)

    def wait_recv(dst, r_at):
        pltpu.make_async_remote_copy(
            dst, dst, ssem.at[0], rsem.at[r_at],
            device_id=c_peer, device_id_type=pl.DeviceIdType.MESH,
        ).wait_recv()

    for k, table in ((0, img), (1, txt)):
        loads[k].wait()
        wide = raw[k].astype(F32)
        norm = jnp.sqrt(jnp.sum(wide * wide, axis=-1, keepdims=True) + EPS)
        units = wide / norm
        unit[k] = units
        length[k] = norm
        table[pl.ds(OWN * ROWS, ROWS)] = units.astype(BF)

    pl.semaphore_wait(barrier, len(peers))

    for s, o in enumerate(OFFS[:-1]):
        t = slot_of(-o)
        send(rows(img, 0, OWN), rows(img, 0, t), GZ + s, GZ + t, z_peer[o])
        send(rows(txt, 0, OWN), rows(txt, 0, t), GY + s, GY + t, y_peer[o])
        if s == 0:
            send(rows(img, 0, OWN), rows(img, 1, OWN), GXI + OWN, GXI + OWN, xa_peer)
            send(rows(txt, 0, OWN), rows(txt, 1, OWN), GXT + OWN, GXT + OWN, xb_peer)
    send(rows(txt, 0, OWN), rows(txt, 2, OWN), GC + OWN, GC + OWN, c_peer)

    for s in reversed(range(OWN)):
        wait_recv(rows(txt, 0, s), GY + s)
        send(rows(txt, 0, s), rows(txt, 1, s), GXT + s, GXT + s, xb_peer)
        send(rows(txt, 0, s), rows(txt, 2, s), GC + s, GC + s, c_peer)
        wait_recv(rows(img, 0, s), GZ + s)
        send(rows(img, 0, s), rows(img, 1, s), GXI + s, GXI + s, xa_peer)
    for s in reversed(range(RING)):
        wait_recv(rows(txt, 1, s), GXT + s)
        send(rows(txt, 1, s), rows(txt, 3, s), GC + RING + s, GC + RING + s, c_peer)
    for s in reversed(range(RING)):
        wait_recv(rows(img, 1, s), GXI + s)
        wait_recv(rows(txt, 2, s), GC + s)
    for s in reversed(range(RING)):
        wait_recv(rows(txt, 3, s), GC + RING + s)

    scale = jnp.exp(jnp.full((1, 1), scale_ref[0], F32))
    offset = bias_ref[0]
    for q in range(4):
        dots = lax.dot_general(
            img[...], txt[pl.ds(q * HALF, HALF)], (((1,), (1,)), ((), ())), preferred_element_type=F32
        )
        prob = jax.nn.sigmoid(scale * dots + offset)
        if q == 0:
            i = lax.broadcasted_iota(jnp.int32, prob.shape, 0)
            j = lax.broadcasted_iota(jnp.int32, prob.shape, 1)
            prob = prob - jnp.where((i == j) & (i >= OWN * ROWS), 1.0, 0.0)
        grad[:, pl.ds(q * HALF, HALF)] = (scale * prob).astype(BF)

    def text_part(q):
        return lax.dot_general(
            grad[:, pl.ds(q * HALF, HALF)], img[...], (((0,), (0,)), ((), ())), preferred_element_type=F32
        )

    def image_part(q):
        return jnp.dot(grad[pl.ds(q * HALF, HALF), :], txt[...], preferred_element_type=F32)

    for h in (1, 0):
        snd_c[pl.ds(h * HALF, HALF)] = text_part(2 + h).astype(BF)
        send(rows(snd_c, h, 0, RING), rows(rcv_c, h, 0, RING), RC + h, RC + h, c_peer)
    snd_xi[...] = image_part(1).astype(BF)
    for b in range(NBATCH):
        part = pl.ds(b * BATCH * ROWS, BATCH * ROWS)
        send(snd_xi.at[part], rcv_xi.at[part], RXI + b, RXI + b, xa_peer)
    own_t[...] = text_part(1)
    wait_recv(rows(rcv_c, 1, 0, RING), RC + 1)
    for b in range(NBATCH):
        part = pl.ds(b * BATCH * ROWS, BATCH * ROWS)
        snd_xt[part] = (own_t[part] + rcv_c[pl.ds(HALF + b * BATCH * ROWS, BATCH * ROWS)].astype(F32)).astype(BF)
        send(snd_xt.at[part], rcv_xt.at[part], RXT + b, RXT + b, xb_peer)
    own_i[...] = image_part(0)
    own_t[...] = text_part(0)
    wait_recv(rows(rcv_c, 0, 0, RING), RC + 0)
    own_t[...] += rcv_c[pl.ds(0, HALF)].astype(F32)
    for b in range(NBATCH):
        part = pl.ds(b * BATCH * ROWS, BATCH * ROWS)
        for own, snd, rcv_x, rcv, sem_x, sem, peer in (
            (own_i, snd_z, rcv_xi, rcv_z, RXI, RZ, z_peer),
            (own_t, snd_y, rcv_xt, rcv_y, RXT, RY, y_peer),
        ):
            wait_recv(rcv_x.at[part], sem_x + b)
            own[part] += rcv_x[part].astype(F32)
            snd[part] = own[part].astype(BF)
            for s in range(b * BATCH, (b + 1) * BATCH):
                if s != OWN:
                    t = slot_of(-OFFS[s])
                    send(rows(snd, 0, s), rows(rcv, 0, t), sem + s, sem + t, peer[OFFS[s]])

    for k, (own, rcv, sem, out) in enumerate(((own_i, rcv_z, RZ, out_i), (own_t, rcv_y, RY, out_t))):
        total = own[pl.ds(OWN * ROWS, ROWS)]
        for s in range(OWN):
            wait_recv(rows(rcv, 0, s), sem + s)
            total = total + rcv[pl.ds(s * ROWS, ROWS)].astype(F32)
        units = unit[k]
        along = jnp.sum(units * total, axis=-1, keepdims=True)
        out[...] = (total - units * along) / length[k]
    for copy in sent:
        copy.wait_send()


def per_device(image_emb, text_emb, log_scale, bias):
    rows, width = image_emb.shape
    out = jax.ShapeDtypeStruct((rows, width), F32)
    vmem = lambda n, dtype: pltpu.VMEM((n, width), dtype)
    return pl.pallas_call(
        kernel,
        out_shape=(out, out),
        in_specs=[pl.BlockSpec(memory_space=pl.ANY)] * 2 + [pl.BlockSpec(memory_space=pltpu.SMEM)] * 2,
        out_specs=(pl.BlockSpec(memory_space=pltpu.VMEM),) * 2,
        scratch_shapes=[
            pltpu.VMEM((2, rows, width), BF),
            pltpu.VMEM((2, rows, width), F32),
            pltpu.VMEM((2, rows, 1), F32),
            vmem(2 * HALF, BF),
            vmem(4 * HALF, BF),
            pltpu.VMEM((2 * HALF, 4 * HALF), BF),
            vmem(HALF, F32),
            vmem(HALF, F32),
            vmem(2 * HALF, BF),
            vmem(HALF, BF),
            vmem(HALF, BF),
            vmem(HALF, BF),
            vmem(HALF, BF),
            vmem(2 * HALF, BF),
            vmem(HALF, BF),
            vmem(HALF, BF),
            vmem(HALF, BF),
            vmem(HALF, BF),
            pltpu.SemaphoreType.DMA((2,)),
            pltpu.SemaphoreType.DMA((NSEM,)),
            pltpu.SemaphoreType.DMA((NSEM,)),
        ],
        compiler_params=pltpu.CompilerParams(
            collective_id=0, has_side_effects=True, vmem_limit_bytes=48 * 2**20
        ),
        name="siglip_grads",
    )(image_emb, text_emb, log_scale, bias)


def solution(mesh):
    return jax.shard_map(
        per_device,
        mesh=mesh,
        in_specs=(P(("loop", "grp"), None), P(("loop", "grp"), None), P(), P()),
        out_specs=(P(("loop", "grp"), None), P(("loop", "grp"), None)),
        check_vma=False,
    )
```

time: 514 us -> 52.8 us (0.10)
  the two profiles are of different devices: /device:TPU:4 before, /device:TPU:1 now
where the time goes in v1:
time: 52.8 us; the launch traced here: 52.5 us
  Pallas kernels  47.8 us (91%)
  local copies, waits for them, and re-layouts  2.8 us (5%)
  between operations  1.94 us (4%)
    pallas_call x1, Pallas kernels, per_device(): pl.pallas_call(kernel, out_shape=(out, out), in_specs=[pl.BlockSpec(memor...  47.8 us
    unnamed x6, local copies, waits for them, and re-layouts  2.8 us

profile of v1, /device:TPU:1, one launch (start us, length us, event | category | flops | bytes accessed | tf_op | source)
XLA Modules:
  0.0 52.5 jit_solution(1666028293184077034)
XLA Ops:
  1.9 0.0 copy-start
  1.9 0.8 %copy-done = bf16[16,1152]{1,0:T(8,128)(2,1)S(1)} copy-done((bf16[16,1152]{1,0:T(8,128)(2,1)S(1)}, bf16[16,1152]{1,0:T(8,128)(2,1)}, u32[]{:S(2)}) %copy-start) | copy-done | bytes 36888
  2.7 0.0 copy-start.1
  2.7 0.8 %copy-done.1 = bf16[16,1152]{1,0:T(8,128)(2,1)S(1)} copy-done((bf16[16,1152]{1,0:T(8,128)(2,1)S(1)}, bf16[16,1152]{1,0:T(8,128)(2,1)}, u32[]{:S(2)}) %copy-start.1) | copy-done | bytes 36888
  3.5 47.8 %siglip_grads.1 = (f32[16,1152]{1,0:T(8,128)S(1)}, f32[16,1152]{1,0:T(8,128)S(1)}) custom-call(bf16[16,1152]{1,0:T(8,128)(2,1)S(1)} %copy-done, bf16[16,1152]{1,0:T(8,128)(2,1)S(1)} %copy-done.1, f32[1]{0:T(128)S(6)} %copy.8.scale_ref, f32[1]{0:T(128)S(6)} %copy.9.bias_ref), custom_call_target="tpu_custom_call" | custom-call | tf_op jit(solution)/shard_map/siglip_grads/pallas_call | solution.py:188
  51.3 0.6 %copy.10 = f32[16,1152]{1,0:T(8,128)} copy(f32[16,1152]{1,0:T(8,128)S(1)} %get-tuple-element.4) | data formatting | bytes 147456
  51.9 0.6 %copy.11 = f32[16,1152]{1,0:T(8,128)} copy(f32[16,1152]{1,0:T(8,128)S(1)} %get-tuple-element.5) | data formatting | bytes 147456
Async XLA Ops:
  1.9 0.8 %copy-start = (bf16[16,1152]{1,0:T(8,128)(2,1)S(1)}, bf16[16,1152]{1,0:T(8,128)(2,1)}, u32[]{:S(2)}) copy-start(bf16[16,1152]{1,0:T(8,128)(2,1)} %img_hbm.1) | copy-start | bytes 110596
  2.7 0.8 %copy-start.1 = (bf16[16,1152]{1,0:T(8,128)(2,1)S(1)}, bf16[16,1152]{1,0:T(8,128)(2,1)}, u32[]{:S(2)}) copy-start(bf16[16,1152]{1,0:T(8,128)(2,1)} %txt_hbm.1) | copy-start | bytes 110596

commit v2 on v1

v2 whole, which is shorter than its diff:
```python
import jax
import jax.numpy as jnp
from jax import lax
from jax.experimental import pallas as pl
from jax.experimental.pallas import tpu as pltpu
from jax.sharding import PartitionSpec as P

EPS = 1e-06
ROWS = 16
RING = 8
OFFS = (4, 3, -3, 2, -2, 1, -1, 0)
OWN = 7
HALF = RING * ROWS
BF = jnp.bfloat16
F32 = jnp.float32


def slot_of(offset):
    return OFFS.index(4 if offset in (4, -4) else offset)


XPARTS = ((1, 3), (3, 8))
GI, GT, GXI, GXT, GC = 0, 8, 16, 24, 32
RC, RXI, RXT, RI, RT, RFI, RFT = 48, 52, 60, 68, 76, 84, 86
NRECV = 88
NSEND = 100


def kernel(
    img_hbm, txt_hbm, scale_ref, bias_ref, out_i, out_t,
    raw, unit, length, img, txt, grad, own_i, own_t,
    snd_c, snd_xi, snd_xt, snd_ri, snd_rt,
    rcv_c, rcv_xi, rcv_xt, rcv_ri, rcv_rt, rcv_fi, rcv_ft,
    in_sem, ssem, rsem,
):
    loop_at = lax.axis_index("loop")
    grp_at = lax.axis_index("grp")
    c = loop_at % 2
    x = (loop_at // 2) % 4
    y_hi = loop_at // 8
    y_lo = grp_at // 8
    z = grp_at % 8
    y = y_hi * 2 + y_lo

    def device(dx, dy, dz, dc):
        return {"loop": ((dy // 2) * 4 + dx) * 2 + dc, "grp": (dy % 2) * 8 + dz}

    i_peer = {o: device(x, (y + o + RING) % RING, z, c) for o in OFFS[1:-1]}
    t_peer = {o: device(x, y, (z + o + RING) % RING, c) for o in OFFS[1:-1]}
    xa = x + 1 - 2 * (x % 2)
    xb = 3 - x
    xa_peer = device(xa, y, z, c)
    xb_peer = device(xb, y, z, c)
    xi_peer = device(xa, (y - 1 + RING) % RING, z, c)
    xt_peer = device(xb, y, (z - 1 + RING) % RING, c)
    xi_from = device(xa, (y + 1) % RING, z, c)
    xt_from = device(xb, y, (z + 1) % RING, c)
    c_peer = device(x, y, z, 1 - c)

    loads = [
        pltpu.make_async_copy(img_hbm, raw.at[0], in_sem.at[0]),
        pltpu.make_async_copy(txt_hbm, raw.at[1], in_sem.at[1]),
    ]
    for load in loads:
        load.start()

    barrier = pltpu.get_barrier_semaphore()
    peers = list(i_peer.values()) + list(t_peer.values()) + [xa_peer, xb_peer, c_peer, xi_peer, xi_from, xt_peer, xt_from]
    for peer in peers:
        pl.semaphore_signal(barrier, 1, device_id=peer, device_id_type=pl.DeviceIdType.MESH)

    def rows(ref, quarter, slot, count=1):
        return ref.at[pl.ds(quarter * HALF + slot * ROWS, count * ROWS)]

    sent = []

    def send(src, dst, r_at, peer):
        copy = pltpu.make_async_remote_copy(
            src, dst, ssem.at[len(sent)], rsem.at[r_at],
            device_id=peer, device_id_type=pl.DeviceIdType.MESH,
        )
        copy.start()
        sent.append(copy)

    def wait_recv(dst, r_at):
        pltpu.make_async_remote_copy(
            dst, dst, ssem.at[0], rsem.at[r_at],
            device_id=c_peer, device_id_type=pl.DeviceIdType.MESH,
        ).wait_recv()

    def normalize(k, table):
        loads[k].wait()
        wide = raw[k].astype(F32)
        norm = jnp.sqrt(jnp.sum(wide * wide, axis=-1, keepdims=True) + EPS)
        units = wide / norm
        unit[k] = units
        length[k] = norm
        table[pl.ds(OWN * ROWS, ROWS)] = units.astype(BF)

    normalize(1, txt)
    normalize(0, img)
    pl.semaphore_wait(barrier, len(peers))
    def text_part(q):
        return lax.dot_general(
            grad[:, pl.ds(q * HALF, HALF)], img[...], (((0,), (0,)), ((), ())), preferred_element_type=F32
        )

    def image_part(q):
        return jnp.dot(grad[pl.ds(q * HALF, HALF), :], txt[...], preferred_element_type=F32)

    def gather():
        send(rows(txt, 0, OWN), rows(txt, 1, OWN), GXT + OWN, xb_peer)
        send(rows(img, 0, OWN), rows(img, 1, OWN), GXI + OWN, xa_peer)
        send(rows(txt, 0, OWN), rows(txt, 2, OWN), GC + OWN, c_peer)
        for s in range(1, OWN):
            o = OFFS[s]
            t = slot_of(-o)
            send(rows(txt, 0, OWN), rows(txt, 0, t), GT + t, t_peer[o])
            send(rows(img, 0, OWN), rows(img, 0, t), GI + t, i_peer[o])
        wait_recv(rows(txt, 0, 1), GT + 1)
        send(rows(txt, 0, 1), rows(txt, 0, 0), GT, t_peer[-1])
        wait_recv(rows(img, 0, 1), GI + 1)
        send(rows(img, 0, 1), rows(img, 0, 0), GI, i_peer[-1])
        parts = ((1, 3), (3, OWN), (0, 1))
        for lo, hi in parts:
            n = hi - lo
            for s in range(lo, hi):
                if s != 1:
                    wait_recv(rows(txt, 0, s), GT + s)
            send(rows(txt, 0, lo, n), rows(txt, 1, lo, n), GXT + lo, xb_peer)
            send(rows(txt, 0, lo, n), rows(txt, 2, lo, n), GC + lo, c_peer)
            for s in range(lo, hi):
                if s != 1:
                    wait_recv(rows(img, 0, s), GI + s)
            send(rows(img, 0, lo, n), rows(img, 1, lo, n), GXI + lo, xa_peer)
        parts = ((OWN, RING), *parts)
        for lo, hi in parts:
            n = hi - lo
            wait_recv(rows(txt, 1, lo, n), GXT + lo)
            send(rows(txt, 1, lo, n), rows(txt, 3, lo, n), GC + RING + lo, c_peer)
        for lo, hi in parts:
            n = hi - lo
            wait_recv(rows(img, 1, lo, n), GXI + lo)
            wait_recv(rows(txt, 2, lo, n), GC + lo)
            wait_recv(rows(txt, 3, lo, n), GC + RING + lo)

    def grads():
        scale = jnp.exp(jnp.full((1, 1), scale_ref[0], F32))
        offset = bias_ref[0]
        for q in range(4):
            dots = lax.dot_general(
                img[...], txt[pl.ds(q * HALF, HALF)], (((1,), (1,)), ((), ())), preferred_element_type=F32
            )
            prob = jax.nn.sigmoid(scale * dots + offset)
            if q == 0:
                i = lax.broadcasted_iota(jnp.int32, prob.shape, 0)
                j = lax.broadcasted_iota(jnp.int32, prob.shape, 1)
                prob = prob - jnp.where((i == j) & (i >= OWN * ROWS), 1.0, 0.0)
            grad[:, pl.ds(q * HALF, HALF)] = (scale * prob).astype(BF)

    def reduce():
        def span(lo, hi):
            return pl.ds(lo * ROWS, (hi - lo) * ROWS)

        def cross(snd, rcv_x, rcv_f, sem_x, sem_f, peer, far_peer):
            send(rows(snd, 0, 0), rows(rcv_f, 0, 1), sem_f + 1, far_peer)
            for lo, hi in XPARTS:
                send(rows(snd, 0, lo, hi - lo), rows(rcv_x, 0, lo, hi - lo), sem_x + lo, peer)

        def far(own, snd, rcv_f, sem_f, peer):
            snd[span(0, 1)] = own[span(0, 1)].astype(BF)
            send(rows(snd, 0, 0), rows(rcv_f, 0, 0), sem_f, peer[1])

        def spread(own, snd, rcv_x, rcv_f, rcv, sem_x, sem_f, sem, peer, lo, hi):
            at = span(lo, hi)
            wait_recv(rcv_x.at[at], sem_x + lo)
            own[at] += rcv_x[at].astype(F32)
            if lo == 1:
                wait_recv(rows(rcv_f, 0, 0), sem_f)
                wait_recv(rows(rcv_f, 0, 1), sem_f + 1)
                own[span(1, 3)] += rcv_f[...].astype(F32)
            snd[at] = own[at].astype(BF)
            for s in range(lo, min(hi, OWN)):
                t = slot_of(-OFFS[s])
                send(rows(snd, 0, s), rows(rcv, 0, t), sem + t, peer[OFFS[s]])

        for h in (1, 0):
            snd_c[pl.ds(h * HALF, HALF)] = text_part(2 + h).astype(BF)
            send(rows(snd_c, h, 0, RING), rows(rcv_c, h, 0, RING), RC + h, c_peer)
        snd_xi[...] = image_part(1).astype(BF)
        cross(snd_xi, rcv_xi, rcv_fi, RXI, RFI, xa_peer, xi_peer)
        own_i[...] = image_part(0)
        far(own_i, snd_ri, rcv_fi, RFI, i_peer)
        own_t[...] = text_part(1)
        wait_recv(rows(rcv_c, 1, 0, RING), RC + 1)
        snd_xt[...] = (own_t[...] + rcv_c[pl.ds(HALF, HALF)].astype(F32)).astype(BF)
        cross(snd_xt, rcv_xt, rcv_ft, RXT, RFT, xb_peer, xt_peer)
        own_t[...] = text_part(0)
        wait_recv(rows(rcv_c, 0, 0, RING), RC + 0)
        own_t[...] += rcv_c[pl.ds(0, HALF)].astype(F32)
        far(own_t, snd_rt, rcv_ft, RFT, t_peer)
        for lo, hi in XPARTS:
            spread(own_i, snd_ri, rcv_xi, rcv_fi, rcv_ri, RXI, RFI, RI, i_peer, lo, hi)
            spread(own_t, snd_rt, rcv_xt, rcv_ft, rcv_rt, RXT, RFT, RT, t_peer, lo, hi)

    def finish():
        for k, (own, rcv, sem, out) in enumerate(((own_i, rcv_ri, RI, out_i), (own_t, rcv_rt, RT, out_t))):
            total = own[pl.ds(OWN * ROWS, ROWS)]
            for s in range(1, OWN):
                wait_recv(rows(rcv, 0, s), sem + s)
                total = total + rcv[pl.ds(s * ROWS, ROWS)].astype(F32)
            units = unit[k]
            along = jnp.sum(units * total, axis=-1, keepdims=True)
            out[...] = (total - units * along) / length[k]
    def drain():
        for copy in sent:
            copy.wait_send()
        sent.clear()

    gather()
    grads()
    reduce()
    finish()
    drain()


def per_device(image_emb, text_emb, log_scale, bias):
    rows, width = image_emb.shape
    out = jax.ShapeDtypeStruct((rows, width), F32)
    vmem = lambda n, dtype: pltpu.VMEM((n, width), dtype)
    return pl.pallas_call(
        kernel,
        out_shape=(out, out),
        in_specs=[pl.BlockSpec(memory_space=pl.ANY)] * 2 + [pl.BlockSpec(memory_space=pltpu.SMEM)] * 2,
        out_specs=(pl.BlockSpec(memory_space=pltpu.VMEM),) * 2,
        scratch_shapes=[
            pltpu.VMEM((2, rows, width), BF),
            pltpu.VMEM((2, rows, width), F32),
            pltpu.VMEM((2, rows, 1), F32),
            vmem(2 * HALF, BF),
            vmem(4 * HALF, BF),
            pltpu.VMEM((2 * HALF, 4 * HALF), BF),
            vmem(HALF, F32),
            vmem(HALF, F32),
            vmem(2 * HALF, BF),
            vmem(HALF, BF),
            vmem(HALF, BF),
            vmem(HALF, BF),
            vmem(HALF, BF),
            vmem(2 * HALF, BF),
            vmem(HALF, BF),
            vmem(HALF, BF),
            vmem(HALF, BF),
            vmem(HALF, BF),
            vmem(2 * ROWS, BF),
            vmem(2 * ROWS, BF),
            pltpu.SemaphoreType.DMA((2,)),
            pltpu.SemaphoreType.DMA((NSEND,)),
            pltpu.SemaphoreType.DMA((NRECV,)),
        ],
        compiler_params=pltpu.CompilerParams(
            collective_id=0, has_side_effects=True, vmem_limit_bytes=48 * 2**20
        ),
        name="siglip_grads",
    )(
        pltpu.with_memory_space_constraint(image_emb, pltpu.HBM),
        pltpu.with_memory_space_constraint(text_emb, pltpu.HBM),
        log_scale,
        bias,
    )


def solution(mesh):
    return jax.shard_map(
        per_device,
        mesh=mesh,
        in_specs=(P(("loop", "grp"), None), P(("loop", "grp"), None), P(), P()),
        out_specs=(P(("loop", "grp"), None), P(("loop", "grp"), None)),
        check_vma=False,
    )
```

time: 52.8 us -> 49.2 us (0.932)
  Pallas kernels: 47.8 us -> 45.8 us
  local copies, waits for them, and re-layouts: 2.8 us -> 1.27 us
    pallas_call x1, Pallas kernels: 47.8 us -> 45.8 us  [per_device(): pl.pallas_call(kernel, out_shape=(out, out), in_specs=[pl.BlockSpec(memor...]
    unnamed x6 -> x2, local copies, waits for them, and re-layouts: 2.8 us -> 1.27 us
where the time goes in v2:
time: 49.2 us; the launch traced here: 49 us
  Pallas kernels  45.8 us (93%)
  between operations  1.93 us (4%)
  local copies, waits for them, and re-layouts  1.27 us (3%)
    pallas_call x1, Pallas kernels, per_device(): pl.pallas_call(kernel, out_shape=(out, out), in_specs=[pl.BlockSpec(memor...  45.8 us
    unnamed x2, local copies, waits for them, and re-layouts  1.27 us

profile of v2, /device:TPU:1, one launch (start us, length us, event | category | flops | bytes accessed | tf_op | source)
XLA Modules:
  0.0 49.0 jit_solution(16507895870261131397)
XLA Ops:
  1.9 45.8 %siglip_grads.1 = (f32[16,1152]{1,0:T(8,128)S(1)}, f32[16,1152]{1,0:T(8,128)S(1)}) custom-call(bf16[16,1152]{1,0:T(8,128)(2,1)} %img_hbm.1, bf16[16,1152]{1,0:T(8,128)(2,1)} %txt_hbm.1, f32[1]{0:T(128)S(6)} %copy.8.scale_ref, f32[1]{0:T(128)S(6)} %copy.9.bias_ref), custom_call_target="tpu_custom_call" | custom-call | tf_op jit(solution)/shard_map/siglip_grads/pallas_call | solution.py:231
  47.7 0.6 %copy.10 = f32[16,1152]{1,0:T(8,128)} copy(f32[16,1152]{1,0:T(8,128)S(1)} %get-tuple-element.4) | data formatting | bytes 147456
  48.3 0.6 %copy.11 = f32[16,1152]{1,0:T(8,128)} copy(f32[16,1152]{1,0:T(8,128)S(1)} %get-tuple-element.5) | data formatting | bytes 147456

commit v3 on v2

v3 whole, which is shorter than its diff:
```python
import jax
import jax.numpy as jnp
from jax import lax
from jax.experimental import pallas as pl
from jax.experimental.pallas import tpu as pltpu
from jax.sharding import PartitionSpec as P

EPS = 1e-06
ROWS = 16
RING = 8
OFFS = (4, 3, -3, 2, -2, 1, -1, 0)
OWN = 7
HALF = RING * ROWS
BF = jnp.bfloat16
F32 = jnp.float32


def slot_of(offset):
    return OFFS.index(4 if offset in (4, -4) else offset)


NEAR = (5, 6, 3, 4)
GI, GT, GXI, GXT, GC = 0, 8, 16, 24, 32
RC, RXI, RXT, RI, RT, RFI, RFT, RDI, RDT = 48, 52, 53, 54, 62, 70, 72, 74, 82
NRECV = 90
NSEND = 100


def kernel(
    img_hbm, txt_hbm, scale_ref, bias_ref, out_i, out_t,
    raw, unit, length, img, txt, grad, own_i, own_t,
    snd_c, snd_xi, snd_xt, snd_ri, snd_rt, snd_li, snd_lt,
    rcv_c, rcv_xi, rcv_xt, rcv_ri, rcv_rt, rcv_fi, rcv_ft, rcv_di, rcv_dt,
    in_sem, ssem, rsem,
):
    loop_at = lax.axis_index("loop")
    grp_at = lax.axis_index("grp")
    c = loop_at % 2
    x = (loop_at // 2) % 4
    y_hi = loop_at // 8
    y_lo = grp_at // 8
    z = grp_at % 8
    y = y_hi * 2 + y_lo

    def device(dx, dy, dz, dc):
        return {"loop": ((dy // 2) * 4 + dx) * 2 + dc, "grp": (dy % 2) * 8 + dz}

    i_peer = {o: device(x, (y + o + RING) % RING, z, c) for o in OFFS[1:-1]}
    t_peer = {o: device(x, y, (z + o + RING) % RING, c) for o in OFFS[1:-1]}
    xa = x + 1 - 2 * (x % 2)
    xb = 3 - x
    xa_peer = device(xa, y, z, c)
    xb_peer = device(xb, y, z, c)
    xi_peer = {o: device(xa, (y + o + RING) % RING, z, c) for o in (1, -1, 2, -2)}
    xt_peer = {o: device(xb, y, (z + o + RING) % RING, c) for o in (1, -1, 2, -2)}
    c_peer = device(x, y, z, 1 - c)

    loads = [
        pltpu.make_async_copy(img_hbm, raw.at[0], in_sem.at[0]),
        pltpu.make_async_copy(txt_hbm, raw.at[1], in_sem.at[1]),
    ]
    for load in loads:
        load.start()

    barrier = pltpu.get_barrier_semaphore()
    peers = []
    for o in (3, -3, 2, -2, 1, -1):
        peers += [table[o] for table in (t_peer, i_peer, xt_peer, xi_peer) if o in table]
    peers += [xb_peer, xa_peer, c_peer]
    for peer in peers:
        pl.semaphore_signal(barrier, 1, device_id=peer, device_id_type=pl.DeviceIdType.MESH)

    def rows(ref, quarter, slot, count=1):
        return ref.at[pl.ds(quarter * HALF + slot * ROWS, count * ROWS)]

    sent = []

    def send(src, dst, r_at, peer):
        copy = pltpu.make_async_remote_copy(
            src, dst, ssem.at[len(sent)], rsem.at[r_at],
            device_id=peer, device_id_type=pl.DeviceIdType.MESH,
        )
        copy.start()
        sent.append(copy)

    def wait_recv(dst, r_at):
        pltpu.make_async_remote_copy(
            dst, dst, ssem.at[0], rsem.at[r_at],
            device_id=c_peer, device_id_type=pl.DeviceIdType.MESH,
        ).wait_recv()

    def normalize(k, table):
        loads[k].wait()
        wide = raw[k].astype(F32)
        norm = jnp.sqrt(jnp.sum(wide * wide, axis=-1, keepdims=True) + EPS)
        units = wide / norm
        unit[k] = units
        length[k] = norm
        table[pl.ds(OWN * ROWS, ROWS)] = units.astype(BF)

    normalize(1, txt)
    pl.semaphore_wait(barrier, len(peers))
    def span(lo, hi):
        return pl.ds(lo * ROWS, (hi - lo) * ROWS)

    def text_part(q, lo, hi):
        part = grad[:, pl.ds(q * HALF + lo * ROWS, (hi - lo) * ROWS)]
        return lax.dot_general(part, img[...], (((0,), (0,)), ((), ())), preferred_element_type=F32)

    def image_part(q, lo, hi):
        part = grad[pl.ds(q * HALF + lo * ROWS, (hi - lo) * ROWS), :]
        return jnp.dot(part, txt[...], preferred_element_type=F32)

    def gather():
        sides = (
            (txt, GT, GXT, t_peer, xt_peer, xb_peer),
            (img, GI, GXI, i_peer, xi_peer, xa_peer),
        )
        for ref, sem, sem_x, ring, diag, pair in sides:
            if ref is img:
                normalize(0, img)
            for s in (1, 2):
                t = slot_of(-OFFS[s])
                send(rows(ref, 0, OWN), rows(ref, 0, t), sem + t, ring[OFFS[s]])
        for ref, sem, sem_x, ring, diag, pair in sides:
            send(rows(ref, 0, OWN), rows(ref, 1, OWN), sem_x + OWN, pair)
        for s in NEAR:
            for ref, sem, sem_x, ring, diag, pair in sides:
                t = slot_of(-OFFS[s])
                send(rows(ref, 0, OWN), rows(ref, 0, t), sem + t, ring[OFFS[s]])
                send(rows(ref, 0, OWN), rows(ref, 1, t), sem_x + t, diag[OFFS[s]])
        for ref, sem, sem_x, ring, diag, pair in sides:
            wait_recv(rows(ref, 0, 1), sem + 1)
            send(rows(ref, 0, 1), rows(ref, 0, 0), sem, ring[-1])
            send(rows(ref, 0, 1), rows(ref, 1, 0), sem_x, diag[-1])
            wait_recv(rows(ref, 0, 2), sem + 2)
            send(rows(ref, 0, 1, 2), rows(ref, 1, 1, 2), sem_x + 1, pair)

        def share(q, lo, n):
            send(rows(txt, q, lo, n), rows(txt, 2 + q, lo, n), GC + q * RING + lo, c_peer)

        share(0, 1, 2)
        for q, sem in ((0, GT), (1, GXT)):
            for s in NEAR:
                wait_recv(rows(txt, q, s), sem + s)
            if q == 1:
                wait_recv(rows(txt, q, OWN), sem + OWN)
            share(q, 3, 5)
        wait_recv(rows(txt, 0, 0), GT)
        share(0, 0, 1)
        wait_recv(rows(txt, 1, 1, 2), GXT + 1)
        share(1, 1, 2)
        wait_recv(rows(txt, 1, 0), GXT)
        share(1, 0, 1)
        for q, sem in ((0, GI), (1, GXI)):
            for s in NEAR:
                wait_recv(rows(img, q, s), sem + s)
            wait_recv(rows(img, q, 0), sem)
        wait_recv(rows(img, 1, OWN), GXI + OWN)
        wait_recv(rows(img, 1, 1, 2), GXI + 1)

    def gather_end():
        for q in (0, 1):
            for lo, n in ((3, 5), (1, 2), (0, 1)):
                wait_recv(rows(txt, 2 + q, lo, n), GC + q * RING + lo)

    def grads():
        scale = jnp.exp(jnp.full((1, 1), scale_ref[0], F32))
        offset = bias_ref[0]
        for q in range(4):
            if q == 2:
                gather_end()
            dots = lax.dot_general(
                img[...], txt[pl.ds(q * HALF, HALF)], (((1,), (1,)), ((), ())), preferred_element_type=F32
            )
            prob = jax.nn.sigmoid(scale * dots + offset)
            if q == 0:
                i = lax.broadcasted_iota(jnp.int32, prob.shape, 0)
                j = lax.broadcasted_iota(jnp.int32, prob.shape, 1)
                prob = prob - jnp.where((i == j) & (i >= OWN * ROWS), 1.0, 0.0)
            grad[:, pl.ds(q * HALF, HALF)] = (scale * prob).astype(BF)

    def reduce():
        def cross_far(snd, rcv_x, rcv_f, sem_x, sem_f, pair, diag):
            send(rows(snd, 0, 1, 2), rcv_x, sem_x, pair)
            send(rows(snd, 0, 0), rows(rcv_f, 0, 1), sem_f + 1, diag[-1])

        def along_far(snd, rcv_f, sem_f, ring):
            send(rows(snd, 0, 0), rows(rcv_f, 0, 0), sem_f, ring[1])

        def near(snd_x, snd, rcv_d, rcv, sem_d, sem, pair, diag, ring):
            for s in NEAR:
                t = slot_of(-OFFS[s])
                send(rows(snd_x, 0, s), rows(rcv_d, 0, t), sem_d + t, diag[OFFS[s]])
                send(rows(snd, 0, s), rows(rcv, 0, t), sem + t, ring[OFFS[s]])
            send(rows(snd_x, 0, OWN), rows(rcv_d, 0, OWN), sem_d + OWN, pair)

        def last(own, snd_l, rcv_x, rcv_f, rcv, sem_x, sem_f, sem, ring):
            wait_recv(rcv_x, sem_x)
            wait_recv(rows(rcv_f, 0, 0), sem_f)
            wait_recv(rows(rcv_f, 0, 1), sem_f + 1)
            snd_l[...] = (own[span(1, 3)] + rcv_x[...].astype(F32) + rcv_f[...].astype(F32)).astype(BF)
            for s in (1, 2):
                t = slot_of(-OFFS[s])
                send(rows(snd_l, 0, s - 1), rows(rcv, 0, t), sem + t, ring[OFFS[s]])

        def core_out(lo, hi, sem):
            for h in (1, 0):
                at = pl.ds(h * HALF + lo * ROWS, (hi - lo) * ROWS)
                snd_c[at] = text_part(2 + h, lo, hi).astype(BF)
                send(snd_c.at[at], rcv_c.at[at], sem + h, c_peer)

        def core_in(h, lo, hi, sem):
            at = pl.ds(h * HALF + lo * ROWS, (hi - lo) * ROWS)
            wait_recv(rcv_c.at[at], sem + h)
            return rcv_c[at].astype(F32)

        far, rest = (0, 3), (3, RING)
        core_out(*far, RC)
        snd_xi[span(*far)] = image_part(1, *far).astype(BF)
        cross_far(snd_xi, rcv_xi, rcv_fi, RXI, RFI, xa_peer, xi_peer)
        own_i[span(*far)] = image_part(0, *far)
        snd_ri[span(0, 1)] = own_i[span(0, 1)].astype(BF)
        along_far(snd_ri, rcv_fi, RFI, i_peer)
        cross_t = text_part(1, *far)
        along_t = text_part(0, *far)
        snd_xt[span(*far)] = (cross_t + core_in(1, *far, RC)).astype(BF)
        cross_far(snd_xt, rcv_xt, rcv_ft, RXT, RFT, xb_peer, xt_peer)
        own_t[span(*far)] = along_t + core_in(0, *far, RC)
        snd_rt[span(0, 1)] = own_t[span(0, 1)].astype(BF)
        along_far(snd_rt, rcv_ft, RFT, t_peer)
        core_out(*rest, RC + 2)
        snd_xi[span(*rest)] = image_part(1, *rest).astype(BF)
        own_i[span(*rest)] = image_part(0, *rest)
        snd_ri[span(*rest)] = own_i[span(*rest)].astype(BF)
        near(snd_xi, snd_ri, rcv_di, rcv_ri, RDI, RI, xa_peer, xi_peer, i_peer)
        snd_xt[span(*rest)] = (text_part(1, *rest) + core_in(1, *rest, RC + 2)).astype(BF)
        own_t[span(*rest)] = text_part(0, *rest) + core_in(0, *rest, RC + 2)
        snd_rt[span(*rest)] = own_t[span(*rest)].astype(BF)
        near(snd_xt, snd_rt, rcv_dt, rcv_rt, RDT, RT, xb_peer, xt_peer, t_peer)
        last(own_i, snd_li, rcv_xi, rcv_fi, rcv_ri, RXI, RFI, RI, i_peer)
        last(own_t, snd_lt, rcv_xt, rcv_ft, rcv_rt, RXT, RFT, RT, t_peer)

    def finish():
        tables = (
            (own_i, rcv_ri, rcv_di, RI, RDI, out_i),
            (own_t, rcv_rt, rcv_dt, RT, RDT, out_t),
        )
        totals = []
        for own, rcv, rcv_d, sem, sem_d, out in tables:
            total = own[pl.ds(OWN * ROWS, ROWS)]
            for s in (OWN, *NEAR):
                wait_recv(rows(rcv_d, 0, s), sem_d + s)
                total = total + rcv_d[pl.ds(s * ROWS, ROWS)].astype(F32)
                if s != OWN:
                    wait_recv(rows(rcv, 0, s), sem + s)
                    total = total + rcv[pl.ds(s * ROWS, ROWS)].astype(F32)
            totals.append(total)
        for k, (own, rcv, rcv_d, sem, sem_d, out) in enumerate(tables):
            total = totals[k]
            for s in (1, 2):
                wait_recv(rows(rcv, 0, s), sem + s)
                total = total + rcv[pl.ds(s * ROWS, ROWS)].astype(F32)
            units = unit[k]
            along = jnp.sum(units * total, axis=-1, keepdims=True)
            out[...] = (total - units * along) / length[k]

    def drain():
        for copy in sent:
            copy.wait_send()
        sent.clear()

    gather()
    grads()
    reduce()
    finish()
    drain()


def per_device(image_emb, text_emb, log_scale, bias):
    rows, width = image_emb.shape
    out = jax.ShapeDtypeStruct((rows, width), F32)
    vmem = lambda n, dtype: pltpu.VMEM((n, width), dtype)
    return pl.pallas_call(
        kernel,
        out_shape=(out, out),
        in_specs=[pl.BlockSpec(memory_space=pl.ANY)] * 2 + [pl.BlockSpec(memory_space=pltpu.SMEM)] * 2,
        out_specs=(pl.BlockSpec(memory_space=pltpu.VMEM),) * 2,
        scratch_shapes=[
            pltpu.VMEM((2, rows, width), BF),
            pltpu.VMEM((2, rows, width), F32),
            pltpu.VMEM((2, rows, 1), F32),
            vmem(2 * HALF, BF),
            vmem(4 * HALF, BF),
            pltpu.VMEM((2 * HALF, 4 * HALF), BF),
            vmem(HALF, F32),
            vmem(HALF, F32),
            vmem(2 * HALF, BF),
            vmem(HALF, BF),
            vmem(HALF, BF),
            vmem(HALF, BF),
            vmem(HALF, BF),
            vmem(2 * ROWS, BF),
            vmem(2 * ROWS, BF),
            vmem(2 * HALF, BF),
            vmem(2 * ROWS, BF),
            vmem(2 * ROWS, BF),
            vmem(HALF, BF),
            vmem(HALF, BF),
            vmem(2 * ROWS, BF),
            vmem(2 * ROWS, BF),
            vmem(HALF, BF),
            vmem(HALF, BF),
            pltpu.SemaphoreType.DMA((2,)),
            pltpu.SemaphoreType.DMA((NSEND,)),
            pltpu.SemaphoreType.DMA((NRECV,)),
        ],
        compiler_params=pltpu.CompilerParams(
            collective_id=0, has_side_effects=True, vmem_limit_bytes=48 * 2**20
        ),
        name="siglip_grads",
    )(
        pltpu.with_memory_space_constraint(image_emb, pltpu.HBM),
        pltpu.with_memory_space_constraint(text_emb, pltpu.HBM),
        log_scale,
        bias,
    )


def solution(mesh):
    return jax.shard_map(
        per_device,
        mesh=mesh,
        in_specs=(P(("loop", "grp"), None), P(("loop", "grp"), None), P(), P()),
        out_specs=(P(("loop", "grp"), None), P(("loop", "grp"), None)),
        check_vma=False,
    )
```

time: 49.2 us -> 46.2 us (0.939)
  Pallas kernels: 45.8 us -> 42.8 us
    pallas_call x1, Pallas kernels: 45.8 us -> 42.8 us  [per_device(): pl.pallas_call(kernel, out_shape=(out, out), in_specs=[pl.BlockSpec(memor...]
where the time goes in v3:
time: 46.2 us; the launch traced here: 46 us
  Pallas kernels  42.8 us (93%)
  between operations  1.93 us (4%)
  local copies, waits for them, and re-layouts  1.27 us (3%)
    pallas_call x1, Pallas kernels, per_device(): pl.pallas_call(kernel, out_shape=(out, out), in_specs=[pl.BlockSpec(memor...  42.8 us
    unnamed x2, local copies, waits for them, and re-layouts  1.27 us

profile of v3, /device:TPU:1, one launch (start us, length us, event | category | flops | bytes accessed | tf_op | source)
XLA Modules:
  0.0 46.0 jit_solution(10548206802670182570)
XLA Ops:
  1.9 42.8 %siglip_grads.1 = (f32[16,1152]{1,0:T(8,128)S(1)}, f32[16,1152]{1,0:T(8,128)S(1)}) custom-call(bf16[16,1152]{1,0:T(8,128)(2,1)} %img_hbm.1, bf16[16,1152]{1,0:T(8,128)(2,1)} %txt_hbm.1, f32[1]{0:T(128)S(6)} %copy.8.scale_ref, f32[1]{0:T(128)S(6)} %copy.9.bias_ref), custom_call_target="tpu_custom_call" | custom-call | tf_op jit(solution)/shard_map/siglip_grads/pallas_call | solution.py:284
  44.7 0.6 %copy.10 = f32[16,1152]{1,0:T(8,128)} copy(f32[16,1152]{1,0:T(8,128)S(1)} %get-tuple-element.4) | data formatting | bytes 147456
  45.4 0.6 %copy.11 = f32[16,1152]{1,0:T(8,128)} copy(f32[16,1152]{1,0:T(8,128)S(1)} %get-tuple-element.5) | data formatting | bytes 147456

commit v4 on v3

--- a/solution.py
+++ b/solution.py
@@ -47,8 +47,8 @@
 
     i_peer = {o: device(x, (y + o + RING) % RING, z, c) for o in OFFS[1:-1]}
     t_peer = {o: device(x, y, (z + o + RING) % RING, c) for o in OFFS[1:-1]}
-    xa = x + 1 - 2 * (x % 2)
-    xb = 3 - x
+    xa = 3 - x
+    xb = x + 1 - 2 * (x % 2)
     xa_peer = device(xa, y, z, c)
     xb_peer = device(xb, y, z, c)
     xi_peer = {o: device(xa, (y + o + RING) % RING, z, c) for o in (1, -1, 2, -2)}
@@ -222,6 +222,7 @@
         own_i[span(*far)] = image_part(0, *far)
         snd_ri[span(0, 1)] = own_i[span(0, 1)].astype(BF)
         along_far(snd_ri, rcv_fi, RFI, i_peer)
+        core_out(*rest, RC + 2)
         cross_t = text_part(1, *far)
         along_t = text_part(0, *far)
         snd_xt[span(*far)] = (cross_t + core_in(1, *far, RC)).astype(BF)
@@ -229,7 +230,6 @@
         own_t[span(*far)] = along_t + core_in(0, *far, RC)
         snd_rt[span(0, 1)] = own_t[span(0, 1)].astype(BF)
         along_far(snd_rt, rcv_ft, RFT, t_peer)
-        core_out(*rest, RC + 2)
         snd_xi[span(*rest)] = image_part(1, *rest).astype(BF)
         own_i[span(*rest)] = image_part(0, *rest)
         snd_ri[span(*rest)] = own_i[span(*rest)].astype(BF)

time: 46.2 us -> 45.4 us (0.983)
  Pallas kernels: 42.8 us -> 42 us
    pallas_call x1, Pallas kernels: 42.8 us -> 42 us  [per_device(): pl.pallas_call(kernel, out_shape=(out, out), in_specs=[pl.BlockSpec(memor...]
where the time goes in v4:
time: 45.4 us; the launch traced here: 45.2 us
  Pallas kernels  42 us (93%)
  between operations  1.93 us (4%)
  local copies, waits for them, and re-layouts  1.27 us (3%)
    pallas_call x1, Pallas kernels, per_device(): pl.pallas_call(kernel, out_shape=(out, out), in_specs=[pl.BlockSpec(memor...  42 us
    unnamed x2, local copies, waits for them, and re-layouts  1.27 us

profile of v4, /device:TPU:1, one launch (start us, length us, event | category | flops | bytes accessed | tf_op | source)
XLA Modules:
  0.0 45.2 jit_solution(14786134158500389516)
XLA Ops:
  1.9 42.0 %siglip_grads.1 = (f32[16,1152]{1,0:T(8,128)S(1)}, f32[16,1152]{1,0:T(8,128)S(1)}) custom-call(bf16[16,1152]{1,0:T(8,128)(2,1)} %img_hbm.1, bf16[16,1152]{1,0:T(8,128)(2,1)} %txt_hbm.1, f32[1]{0:T(128)S(6)} %copy.8.scale_ref, f32[1]{0:T(128)S(6)} %copy.9.bias_ref), custom_call_target="tpu_custom_call" | custom-call | tf_op jit(solution)/shard_map/siglip_grads/pallas_call | solution.py:284
  43.9 0.6 %copy.10 = f32[16,1152]{1,0:T(8,128)} copy(f32[16,1152]{1,0:T(8,128)S(1)} %get-tuple-element.4) | data formatting | bytes 147456
  44.6 0.6 %copy.11 = f32[16,1152]{1,0:T(8,128)} copy(f32[16,1152]{1,0:T(8,128)S(1)} %get-tuple-element.5) | data formatting | bytes 147456

commit v5 on v4

--- a/solution.py
+++ b/solution.py
@@ -21,14 +21,14 @@
 
 NEAR = (5, 6, 3, 4)
 GI, GT, GXI, GXT, GC = 0, 8, 16, 24, 32
-RC, RXI, RXT, RI, RT, RFI, RFT, RDI, RDT = 48, 52, 53, 54, 62, 70, 72, 74, 82
-NRECV = 90
+RC, RXI, RXT, RI, RT, RFI, RFT, RDI, RDT = 48, 52, 54, 56, 64, 72, 74, 76, 84
+NRECV = 92
 NSEND = 100
 
 
 def kernel(
-    img_hbm, txt_hbm, scale_ref, bias_ref, out_i, out_t,
-    raw, unit, length, img, txt, grad, own_i, own_t,
+    img_hbm, txt_hbm, scale_ref, bias_ref, sums, unit, length,
+    raw, img, txt, grad, own_i, own_t,
     snd_c, snd_xi, snd_xt, snd_ri, snd_rt, snd_li, snd_lt,
     rcv_c, rcv_xi, rcv_xt, rcv_ri, rcv_rt, rcv_fi, rcv_ft, rcv_di, rcv_dt,
     in_sem, ssem, rsem,
@@ -182,25 +182,26 @@
 
     def reduce():
         def cross_far(snd, rcv_x, rcv_f, sem_x, sem_f, pair, diag):
-            send(rows(snd, 0, 1, 2), rcv_x, sem_x, pair)
             send(rows(snd, 0, 0), rows(rcv_f, 0, 1), sem_f + 1, diag[-1])
+            for s in (1, 2):
+                send(rows(snd, 0, s), rows(rcv_x, 0, s - 1), sem_x + s - 1, pair)
 
         def along_far(snd, rcv_f, sem_f, ring):
             send(rows(snd, 0, 0), rows(rcv_f, 0, 0), sem_f, ring[1])
 
         def near(snd_x, snd, rcv_d, rcv, sem_d, sem, pair, diag, ring):
-            for s in NEAR:
+            for s in (3, 4, 5, 6):
                 t = slot_of(-OFFS[s])
                 send(rows(snd_x, 0, s), rows(rcv_d, 0, t), sem_d + t, diag[OFFS[s]])
                 send(rows(snd, 0, s), rows(rcv, 0, t), sem + t, ring[OFFS[s]])
             send(rows(snd_x, 0, OWN), rows(rcv_d, 0, OWN), sem_d + OWN, pair)
 
         def last(own, snd_l, rcv_x, rcv_f, rcv, sem_x, sem_f, sem, ring):
-            wait_recv(rcv_x, sem_x)
-            wait_recv(rows(rcv_f, 0, 0), sem_f)
-            wait_recv(rows(rcv_f, 0, 1), sem_f + 1)
-            snd_l[...] = (own[span(1, 3)] + rcv_x[...].astype(F32) + rcv_f[...].astype(F32)).astype(BF)
             for s in (1, 2):
+                at = span(s - 1, s)
+                wait_recv(rows(rcv_f, 0, s - 1), sem_f + s - 1)
+                wait_recv(rcv_x.at[at], sem_x + s - 1)
+                snd_l[at] = (own[span(s, s + 1)] + rcv_x[at].astype(F32) + rcv_f[at].astype(F32)).astype(BF)
                 t = slot_of(-OFFS[s])
                 send(rows(snd_l, 0, s - 1), rows(rcv, 0, t), sem + t, ring[OFFS[s]])
 
@@ -243,11 +244,11 @@
 
     def finish():
         tables = (
-            (own_i, rcv_ri, rcv_di, RI, RDI, out_i),
-            (own_t, rcv_rt, rcv_dt, RT, RDT, out_t),
+            (own_i, rcv_ri, rcv_di, RI, RDI),
+            (own_t, rcv_rt, rcv_dt, RT, RDT),
         )
         totals = []
-        for own, rcv, rcv_d, sem, sem_d, out in tables:
+        for own, rcv, rcv_d, sem, sem_d in tables:
             total = own[pl.ds(OWN * ROWS, ROWS)]
             for s in (OWN, *NEAR):
                 wait_recv(rows(rcv_d, 0, s), sem_d + s)
@@ -256,14 +257,12 @@
                     wait_recv(rows(rcv, 0, s), sem + s)
                     total = total + rcv[pl.ds(s * ROWS, ROWS)].astype(F32)
             totals.append(total)
-        for k, (own, rcv, rcv_d, sem, sem_d, out) in enumerate(tables):
+        for k, (own, rcv, rcv_d, sem, sem_d) in enumerate(tables):
             total = totals[k]
             for s in (1, 2):
                 wait_recv(rows(rcv, 0, s), sem + s)
                 total = total + rcv[pl.ds(s * ROWS, ROWS)].astype(F32)
-            units = unit[k]
-            along = jnp.sum(units * total, axis=-1, keepdims=True)
-            out[...] = (total - units * along) / length[k]
+            sums[k] = total
 
     def drain():
         for copy in sent:
@@ -277,19 +276,31 @@
     drain()
 
 
+def project(sums, unit, length, out_i, out_t, rows, sem):
+    copies = []
+    for k, out in enumerate((out_i, out_t)):
+        units = unit[k]
+        total = sums[k]
+        along = jnp.sum(units * total, axis=-1, keepdims=True)
+        rows[k] = (total - units * along) / length[k]
+        copies.append(pltpu.make_async_copy(rows.at[k], out, sem.at[k]))
+        copies[k].start()
+    for copy in copies:
+        copy.wait()
+
+
 def per_device(image_emb, text_emb, log_scale, bias):
     rows, width = image_emb.shape
     out = jax.ShapeDtypeStruct((rows, width), F32)
     vmem = lambda n, dtype: pltpu.VMEM((n, width), dtype)
-    return pl.pallas_call(
+    wide = jax.ShapeDtypeStruct((2, rows, width), F32)
+    parts = pl.pallas_call(
         kernel,
-        out_shape=(out, out),
+        out_shape=(wide, wide, jax.ShapeDtypeStruct((2, rows, 1), F32)),
         in_specs=[pl.BlockSpec(memory_space=pl.ANY)] * 2 + [pl.BlockSpec(memory_space=pltpu.SMEM)] * 2,
-        out_specs=(pl.BlockSpec(memory_space=pltpu.VMEM),) * 2,
+        out_specs=(pl.BlockSpec(memory_space=pltpu.VMEM),) * 3,
         scratch_shapes=[
             pltpu.VMEM((2, rows, width), BF),
-            pltpu.VMEM((2, rows, width), F32),
-            pltpu.VMEM((2, rows, 1), F32),
             vmem(2 * HALF, BF),
             vmem(4 * HALF, BF),
             pltpu.VMEM((2 * HALF, 4 * HALF), BF),
@@ -325,6 +336,14 @@
         log_scale,
         bias,
     )
+    return pl.pallas_call(
+        project,
+        out_shape=(out, out),
+        in_specs=[pl.BlockSpec(memory_space=pltpu.VMEM)] * 3,
+        out_specs=(pl.BlockSpec(memory_space=pltpu.HBM),) * 2,
+        scratch_shapes=[pltpu.VMEM((2, rows, width), F32), pltpu.SemaphoreType.DMA((2,))],
+        name="project",
+    )(*[pltpu.with_memory_space_constraint(part, pltpu.VMEM) for part in parts])
 
 
 def solution(mesh):

time: 45.4 us -> 44.1 us (0.971); the launches traced: 45.2 us -> 43.3 us
  local copies, waits for them, and re-layouts: 1.27 us -> 0 us
  Pallas kernels: 42 us -> 41.3 us
    unnamed x2 -> x0, local copies, waits for them, and re-layouts: 1.27 us -> none
    pallas_call x1 -> x2, Pallas kernels: 42 us -> 41.3 us  [the longest x1 40.6 us: per_device(): pl.pallas_call(kernel, out_shape=(wide, wide, jax.ShapeDtypeStruct((2, ro...]
where the time goes in v5:
time: 44.1 us; the launch traced here: 43.3 us
  Pallas kernels  41.3 us (94%)
  between operations  1.93 us (4%)
    pallas_call x1, Pallas kernels, per_device(): pl.pallas_call(kernel, out_shape=(wide, wide, jax.ShapeDtypeStruct((2, ro...  40.6 us

profile of v5, /device:TPU:1, one launch (start us, length us, event | category | flops | bytes accessed | tf_op | source)
XLA Modules:
  0.0 43.3 jit_solution(13788458498400945420)
XLA Ops:
  1.9 40.6 %siglip_grads.1 = (f32[2,16,1152]{2,1,0:T(8,128)S(1)}, f32[2,16,1152]{2,1,0:T(8,128)S(1)}, f32[2,16,1]{2,1,0:T(8,128)S(1)}) custom-call(bf16[16,1152]{1,0:T(8,128)(2,1)} %img_hbm.1, bf16[16,1152]{1,0:T(8,128)(2,1)} %txt_hbm.1, f32[1]{0:T(128)S(6)} %copy.6.scale_ref, f32[1]{0:T(128)S(6)} %copy.7.bias_ref), custom_call_target="tpu_custom_call" | custom-call | tf_op jit(solution)/shard_map/siglip_grads/pallas_call | solution.py:297
  42.5 0.8 %project.1 = (f32[16,1152]{1,0:T(8,128)}, f32[16,1152]{1,0:T(8,128)}) custom-call(f32[2,16,1152]{2,1,0:T(8,128)S(1)} %get-tuple-element.5.sums, f32[2,16,1152]{2,1,0:T(8,128)S(1)} %get-tuple-element.6.unit, f32[2,16,1]{2,1,0:T(8,128)S(1)} %get-tuple-element.7.length), custom_call_target="tpu_custom_call" | custom-call | tf_op jit(solution)/shard_map/project/pallas_call | solution.py:339
